TPU v7x, 512 devices: a whole 4x4x16 slice. The times are simulated.
512 devices in a mesh: blk: 8 (over z_hi, y), grp: 64 (over x, z_lo, core).
Axes of the slice: x: 4, y: 4, z: 16 (z_hi: 2, z_lo: 8; z = z_hi * 8 + z_lo), core: 2. Of those that a mesh axis runs over, the one named last changes fastest.
Arguments:
- image_emb: bfloat16 [12288, 1152], P('grp'), may hold values from -0.19921875 to 0.19921875
- text_emb: bfloat16 [12288, 1152], P(('blk', 'grp')), may hold values from -0.19921875 to 0.19921875
- log_temp: float32 [1], replicated, may hold values from 0.5 to 1.5
- bias: float32 [1], replicated, may hold values from -3 to -1
Outputs:
- loss: float32 [1], replicated
- grad_image: float32 [12288, 1152], P('grp', 'blk')
- grad_text: float32 [12288, 1152], P(('blk', 'grp'))
- grad_log_temp: float32 [1], replicated
- grad_bias: float32 [1], replicated
All inputs are finite; a program needn't handle non-finite values.
Results may differ from a plain program's by a relative error of at most 0.0038.
The roundings to bfloat16 on the way count: a program that leaves them out, or rounds other values in their place, can miss the bound.
Values may be sent and summed in bfloat16 or wider, within the bound.
A program may use at most 64 MiB of HBM per device.

v0:
```python
import jax
import jax.numpy as jnp
from jax import lax
from jax.experimental import pallas as pl
from jax.experimental.pallas import tpu as pltpu
from jax.sharding import PartitionSpec as P

MESH = pl.DeviceIdType.MESH
epsilon = 1e-06

NX, NY, NZ, ZLO = 4, 4, 16, 8
D = 1152
ROWS = 192
QUARTER = ROWS // NY
IMAGES = ZLO * QUARTER
TEXTS = 24
SLOTS = NX * NY
OWN = SLOTS * TEXTS
COLUMNS = 2 * OWN
GROUP = 4 * TEXTS
LANES = 128
TILES = D // LANES
PACKED = 224
WIDE = D // 2
SLOT = D // 8
BATCH = 12288
STRIDE = 2
Z_SIDES = ((-1, 8), (1, 7))
ORDER = (0, 1, 7, 2, 6, 3, 5, 4)
NEAR = 3
COPIES = 3 + 4 + 12 + 7 + 15 + 4 + 6 + 3 + 3 + 13
F32, BF16 = jnp.float32, jnp.bfloat16
VMEM_LIMIT = 48 * 1024 * 1024


class Peers:
    def __init__(self):
        blk, grp = lax.axis_index("blk"), lax.axis_index("grp")
        z_hi, self.y = blk // NY, blk % NY
        self.core, z_lo, self.x = grp % 2, (grp // 2) % ZLO, grp // (2 * ZLO)
        self.z = z_hi * ZLO + z_lo
        self.sign = 1 - 2 * self.core

    def at(self, x, y, z, core):
        return ((z // ZLO) * NY + y, (x * ZLO + z % ZLO) * 2 + core)

    def other_core(self):
        return self.at(self.x, self.y, self.z, 1 - self.core)

    def along_x(self, step):
        return self.at((self.x + step) % NX, self.y, self.z, self.core)

    def along_y(self, step):
        return self.at(self.x, (self.y + step) % NY, self.z, self.core)

    def first_axis(self, step):
        return self.at(
            (self.x + step * (1 - self.core)) % NX,
            (self.y + step * self.core) % NY,
            self.z,
            self.core,
        )

    def second_axis(self, step):
        return self.at(
            (self.x + step * self.core) % NX,
            (self.y + step * (1 - self.core)) % NY,
            self.z,
            self.core,
        )

    def z_of(self, step):
        return (self.z + self.sign * step + NZ) % NZ

    def along_z(self, step):
        return self.at(self.x, self.y, self.z_of(step), self.core)


class Copies:
    def __init__(self, send_sem, recv_sem):
        self.send_sem, self.recv_sem, self.made = send_sem, recv_sem, []
        self.sent = 0

    def start(self, source, target, device_id):
        at = len(self.made)
        copy = pltpu.make_async_remote_copy(
            src_ref=source,
            dst_ref=target,
            send_sem=self.send_sem.at[at],
            recv_sem=self.recv_sem.at[at],
            device_id=device_id,
            device_id_type=MESH,
        )
        copy.start()
        self.made.append(copy)
        return copy

    def finish(self):
        for copy in self.made[self.sent :]:
            copy.wait_send()
        self.sent = len(self.made)


def pack(rows):
    pieces = [rows[:, k * LANES : (k + 1) * LANES] for k in range(TILES)]
    pieces.append(jnp.zeros((PACKED - TILES * TEXTS, LANES), F32))
    return jnp.concatenate(pieces, axis=0)


def unpack(packed):
    return jnp.concatenate(
        [packed[k * TEXTS : (k + 1) * TEXTS, :] for k in range(TILES)], axis=1
    )


def row_inverse(values):
    return lax.rsqrt(jnp.sum(values * values, axis=1, keepdims=True) + epsilon)


def narrow(rows):
    pieces = [rows[8 * k : 8 * k + 8, LANES:] for k in range(QUARTER // 8)]
    pieces.append(jnp.zeros((8, LANES - (SLOT - LANES) * QUARTER // 8), F32))
    return jnp.concatenate([rows[:, :LANES], jnp.concatenate(pieces, axis=1)], axis=0)


def widen(packed):
    rest = SLOT - LANES
    pieces = [packed[QUARTER:, rest * k : rest * (k + 1)] for k in range(QUARTER // 8)]
    return jnp.concatenate([packed[:QUARTER, :], jnp.concatenate(pieces, axis=0)], axis=1)


def hop(distance):
    return distance % STRIDE or STRIDE


def aligned(start, size):
    return pl.ds(pl.multiple_of(start, size), size)


def kernel(
    log_temp_in,
    bias_in,
    image_in,
    text_in,
    grad_image,
    grad_text,
    totals,
    log_temp,
    bias,
    image,
    text,
    images,
    own_texts,
    other_texts,
    text_bf,
    image_bf,
    similar,
    weights,
    grads,
    halves,
    text_part,
    core_send,
    core_land,
    b_send,
    b_land,
    a_send,
    a_land,
    z_send,
    z_land,
    y_send,
    y_land,
    s_send,
    s_land,
    send_sem,
    recv_sem,
    local_sem,
):
    peers = Peers()
    copies = Copies(send_sem, recv_sem)
    x, y, z, core = peers.x, peers.y, peers.z, peers.core

    image_copy = pltpu.make_async_copy(image_in, image, local_sem.at[0])
    text_copy = pltpu.make_async_copy(text_in, text, local_sem.at[1])
    scalar_copies = [
        pltpu.make_async_copy(log_temp_in, log_temp, local_sem.at[2]),
        pltpu.make_async_copy(bias_in, bias, local_sem.at[3]),
    ]
    for copy in (text_copy, image_copy, *scalar_copies):
        copy.start()
    barrier = pltpu.get_barrier_semaphore()
    met = (
        [peers.other_core()]
        + [peers.along_x(step) for step in range(1, NX)]
        + [peers.along_y(step) for step in range(1, NY)]
        + [peers.along_z(step) for step in (-4, -3, -2, -1, 1, 2, 3, 4, 8)]
    )
    for device_id in met:
        pl.semaphore_signal(barrier, inc=1, device_id=device_id, device_id_type=MESH)
    text_copy.wait()
    own_texts[0] = pack(text[...].astype(F32)).astype(BF16)
    image_copy.wait()
    images[0] = image[aligned(y * QUARTER, QUARTER), :]
    for copy in scalar_copies:
        copy.wait()
    pl.semaphore_wait(barrier, len(met))

    crossing, over_core, over_z = {}, {}, {}

    def text_forward(b):
        slots = pl.ds(4 * b, 4)
        over_core[b] = copies.start(
            own_texts.at[slots], other_texts.at[slots], peers.other_core()
        )

    def text_spread(a):
        crossing[a, 1] = copies.start(own_texts.at[a], own_texts.at[4 + a], peers.second_axis(3))
        crossing[a, 3] = copies.start(own_texts.at[a], own_texts.at[12 + a], peers.second_axis(1))

    def image_forward(distance, side):
        source = (distance if side > 0 else ZLO - distance) % ZLO
        target = (distance + 1 if side > 0 else ZLO - distance - 1) % ZLO
        over_z[target] = copies.start(
            images.at[ORDER.index(source)], images.at[ORDER.index(target)], peers.along_z(-side)
        )

    crossing[1, 0] = copies.start(own_texts.at[0], own_texts.at[1], peers.first_axis(3))
    crossing[3, 0] = copies.start(own_texts.at[0], own_texts.at[3], peers.first_axis(1))
    crossing[2, 0] = copies.start(own_texts.at[0], own_texts.at[2], peers.first_axis(2))
    image_forward(0, 1)
    image_forward(0, -1)
    text_spread(0)

    def image_ready(place):
        rows = pl.ds(place * QUARTER, QUARTER)
        values = images[place].astype(F32)
        image_bf[rows, :] = (values * row_inverse(values)).astype(BF16)

    def texts_ready(texts, b, first):
        for half in range(2):
            slot = b * 4 + 2 * half
            rows = jnp.concatenate(
                [unpack(texts[slot + k].astype(F32)) for k in range(2)], axis=0
            )
            text_bf[pl.ds(first + slot * TEXTS, 2 * TEXTS), :] = (
                rows * row_inverse(rows)
            ).astype(BF16)

    image_ready(0)
    for a in (1, 3, 2):
        crossing[a, 0].wait_recv()
        text_spread(a)
    text_forward(0)
    for target, side in ((1, 1), (7, -1)):
        over_z[target].wait_recv()
        image_forward(1, side)
    texts_ready(own_texts, 0, 0)
    image_ready(1)
    image_ready(2)
    for a in (0, 1, 3, 2):
        for b in (1, 3):
            crossing[a, b].wait_recv()
            if (b == 1) == (a in (0, 3)):
                step = 3 if b == 1 else 1
                crossing[a, 2] = copies.start(
                    own_texts.at[b * 4 + a], own_texts.at[8 + a], peers.second_axis(step)
                )
    text_forward(1)
    text_forward(3)
    for target, side in ((2, 1), (6, -1)):
        over_z[target].wait_recv()
        image_forward(2, side)
    texts_ready(own_texts, 1, 0)
    texts_ready(own_texts, 3, 0)

    def others_ready(b):
        over_core[b].wait_recv()
        texts_ready(other_texts, b, OWN)

    others_ready(0)
    for a in (0, 1, 3, 2):
        crossing[a, 2].wait_recv()
    text_forward(2)
    texts_ready(own_texts, 2, 0)
    others_ready(1)
    others_ready(3)

    scale = jnp.exp(jnp.full((1, 1), log_temp[0], F32))
    shift = bias[0]
    column = lax.broadcasted_iota(jnp.int32, (1, COLUMNS), 1)
    block = (column * 2731) >> 16
    text_core = ((block >> 4) + core) & 1
    on_first, on_second = block & 3, (block >> 2) & 3
    text_x = (x + jnp.where(text_core == 0, on_first, on_second)) & (NX - 1)
    text_y = (y + jnp.where(text_core == 0, on_second, on_first)) & (NY - 1)
    text_ids = (
        ((z // ZLO) * NY + text_y) * (BATCH // 8)
        + ((text_x * ZLO + z % ZLO) * 2 + text_core) * TEXTS
        + column
        - block * TEXTS
    )

    def weigh(low, high, lanes, carry):
        rows = pl.ds(low * QUARTER, (high - low) * QUARTER)
        similar[rows, lanes] = lax.dot_general(
            image_bf[rows, :],
            text_bf[lanes, :],
            (((1,), (1,)), ((), ())),
            preferred_element_type=F32,
        )
        ids = text_ids[:, lanes.start : lanes.start + lanes.size]

        def step(place, carry):
            losses, dlogits, weighted = carry
            rows = aligned(place * QUARTER, QUARTER)
            distance = ((place + 1) // 2) * (2 * (place % 2) - 1)
            image_z = (z + peers.sign * distance + NZ) % ZLO
            first = ((x * ZLO + image_z) * 2 + core) * ROWS + y * QUARTER
            same = first + lax.broadcasted_iota(jnp.int32, (QUARTER, 1), 0) == ids
            product = similar[rows, lanes]
            logits = scale * product + shift
            power = jnp.exp(jnp.where(same, -logits, logits))
            above = 1.0 + power
            chance = power / above
            dlogit = jnp.where(same, -chance, chance)
            weights[rows, lanes] = (scale * dlogit).astype(BF16)
            losses = losses + jnp.sum(jnp.log(above), axis=0, keepdims=True)
            dlogits = dlogits + jnp.sum(dlogit, axis=0, keepdims=True)
            weighted = weighted + jnp.sum(dlogit * product, axis=0, keepdims=True)
            return losses, dlogits, weighted

        return lax.fori_loop(low, high, step, carry)

    def project(place):
        values = images[place].astype(F32)
        unit = values * row_inverse(values)
        grad = grads[aligned(place * QUARTER, QUARTER), :]
        grad = grad - unit * jnp.sum(unit * grad, axis=1, keepdims=True)
        halves[place, 0] = grad[:, :WIDE]
        halves[place, 1] = grad[:, WIDE:]

    def image_grads(low, high):
        rows = pl.ds(low * QUARTER, (high - low) * QUARTER)
        grads[rows, :] = jnp.dot(weights[rows, :], text_bf[...], preferred_element_type=F32)
        pl.loop(low, high)(project)

    index = {}
    for side, most in Z_SIDES:
        for far in range(most, 0, -1):
            index[side, far] = len(index)
    flying = {}

    def part(step):
        return halves[ORDER.index(step % ZLO), peers.z_of(step) // ZLO]

    def gathered(side, most, to, value):
        for far in range(to + 1, min(to + STRIDE, most) + 1):
            flying[side, far].wait_recv()
            value = value + z_land[index[side, far]].astype(F32)
        return value

    def z_start(far):
        for side, most in Z_SIDES:
            if far > most:
                continue
            value = part(side * far)
            if far % STRIDE == 0:
                value = gathered(side, most, far, value)
            at = index[side, far]
            z_send[at] = value.astype(BF16)
            flying[side, far] = copies.start(
                z_send.at[at], z_land.at[at], peers.along_z(side * hop(far))
            )

    scalar = {"stage": 0, "slot": 0, "value": None}

    def scalar_send(value, to):
        stage = scalar["stage"]
        scalar["value"] = value
        s_send[stage] = value
        made = []
        for peer in to:
            slot = scalar["slot"]
            made.append((copies.start(s_send.at[stage], s_land.at[slot], peer), slot))
            scalar["slot"] += 1
        scalar["stage"] += 1
        return made

    def scalar_sum(made):
        value = scalar["value"]
        for copy, slot in made:
            copy.wait_recv()
            value = value + s_land[slot]
        return value

    own_lanes, other_lanes = pl.ds(0, OWN), pl.ds(OWN, OWN)
    zero = jnp.zeros((1, OWN), F32)
    carry = weigh(0, NEAR, own_lanes, (zero, zero, zero))
    over_z[3].wait_recv()
    image_forward(3, 1)
    others_ready(2)
    carry = weigh(0, NEAR, other_lanes, carry)
    image_grads(0, NEAR)
    for far in (8, 7, 1):
        z_start(far)
    for place in (3, 4, 5):
        image_ready(place)
    over_z[5].wait_recv()
    image_ready(6)
    over_z[4].wait_recv()
    image_ready(7)
    wide_zero = jnp.zeros((1, COLUMNS), F32)
    late = weigh(NEAR, ZLO, pl.ds(0, COLUMNS), (wide_zero, wide_zero, wide_zero))

    row = lax.broadcasted_iota(jnp.int32, (8, LANES), 0)
    total = jnp.zeros((8, LANES), F32)
    for k in range(3):
        part_sum = jnp.sum(carry[k], axis=1, keepdims=True)
        part_sum = part_sum + jnp.sum(late[k], axis=1, keepdims=True)
        total = jnp.where(row == k, part_sum, total)
    made = scalar_send(total, [peers.other_core()])

    def text_product(lanes):
        text_part[lanes, :] = lax.dot_general(
            weights[:, lanes],
            image_bf[...],
            (((0,), (0,)), ((), ())),
            preferred_element_type=F32,
        )

    text_product(other_lanes)
    pairs = {}
    for b in (2, 1, 3, 0):
        core_send[b] = text_part[pl.ds(OWN + b * GROUP, GROUP), :].astype(BF16)
        pairs[b] = copies.start(core_send.at[b], core_land.at[b], peers.other_core())
    image_grads(NEAR, ZLO)
    for far in (6, 5, 3):
        z_start(far)
    made = scalar_send(scalar_sum(made), [peers.along_x(step) for step in range(1, NX)])
    text_product(own_lanes)
    made = scalar_send(scalar_sum(made), [peers.along_y(step) for step in range(1, NY)])

    def pair_sum(b):
        pairs[b].wait_recv()
        return text_part[pl.ds(b * GROUP, GROUP), :] + core_land[b].astype(F32)

    across = {}

    def b_start(at, value, step):
        b_send[at] = value.astype(BF16)
        across[at] = copies.start(b_send.at[at], b_land.at[at], peers.second_axis(step))

    def b_landed(at):
        across[at].wait_recv()
        return b_land[at].astype(F32)

    low, high = slice(0, GROUP // 2), slice(GROUP // 2, GROUP)
    opposite = pair_sum(2)
    b_start(0, opposite[low], 1)
    b_start(1, opposite[high], 3)
    above, below = pair_sum(1), pair_sum(3)
    b_start(2, above[high], 1)
    b_start(3, below[low], 3)
    text_sum = pair_sum(0)
    made = scalar_send(scalar_sum(made), [peers.along_z(step) for step in (4, 8, -4)])
    z_start(4)
    b_start(4, above[low] + b_landed(0), 1)
    b_start(5, below[high] + b_landed(1), 3)
    z_start(2)
    text_sum = jnp.concatenate(
        [
            text_sum[low] + b_landed(3) + b_landed(4),
            text_sum[high] + b_landed(2) + b_landed(5),
        ],
        axis=0,
    )
    last = []
    for a in (2, 1, 3):
        a_send[a - 1] = pack(text_sum[a * TEXTS : (a + 1) * TEXTS, :]).astype(BF16)
        last.append((copies.start(a_send.at[a - 1], a_land.at[3 - a], peers.first_axis(a)), 3 - a))
    text_sum = pack(text_sum[:TEXTS, :])
    text_values = text[...].astype(F32)
    text_inverse = row_inverse(text_values)
    text_unit = text_values * text_inverse
    made = scalar_send(scalar_sum(made), [peers.along_z(step) for step in (1, 2, 3)])
    quarters = [aligned(((y + k) % NY) * QUARTER, QUARTER) for k in range(NY)]
    inverses = [row_inverse(image[rows, :].astype(F32)) for rows in quarters]

    grad = part(0)
    for side, most in Z_SIDES:
        grad = gathered(side, most, 0, grad)
    for k in range(NY):
        y_send[k] = narrow(grad[:, k * SLOT : (k + 1) * SLOT])
    over_y = {}
    for step in (2, 1, 3):
        over_y[NY - step] = copies.start(
            y_send.at[(y + step) % NY], y_land.at[NY - step - 1], peers.along_y(step)
        )
    grad_image[quarters[0], :] = widen(y_send[y]) * inverses[0]
    copies.finish()

    for copy, slot in last:
        copy.wait_recv()
        text_sum = text_sum + a_land[slot].astype(F32)
    text_sum = unpack(text_sum)
    inner = jnp.sum(text_unit * text_sum, axis=1, keepdims=True)
    grad_text[...] = (text_sum - text_unit * inner) * text_inverse
    for k in range(1, NY):
        over_y[k].wait_recv()
        grad_image[quarters[k], :] = widen(y_land[k - 1]) * inverses[k]
    factor = jnp.where(row == 0, 1.0 / BATCH, jnp.where(row == 2, scale, 1.0))
    totals[...] = scalar_sum(made) * factor
    copies.finish()


def shards(image_emb, text_emb, log_temp, bias):
    vmem = pl.BlockSpec(memory_space=pltpu.VMEM)
    anywhere = pl.BlockSpec(memory_space=pl.ANY)
    grad_image, grad_text, totals = pl.pallas_call(
        kernel,
        out_shape=(
            jax.ShapeDtypeStruct((ROWS, SLOT), F32),
            jax.ShapeDtypeStruct((TEXTS, D), F32),
            jax.ShapeDtypeStruct((8, LANES), F32),
        ),
        in_specs=[anywhere] * 4,
        out_specs=(vmem,) * 3,
        scratch_shapes=[
            pltpu.SMEM((1,), F32),
            pltpu.SMEM((1,), F32),
            pltpu.VMEM((ROWS, D), BF16),
            pltpu.VMEM((TEXTS, D), BF16),
            pltpu.VMEM((ZLO, QUARTER, D), BF16),
            pltpu.VMEM((SLOTS, PACKED, LANES), BF16),
            pltpu.VMEM((SLOTS, PACKED, LANES), BF16),
            pltpu.VMEM((COLUMNS, D), BF16),
            pltpu.VMEM((IMAGES, D), BF16),
            pltpu.VMEM((IMAGES, COLUMNS), F32),
            pltpu.VMEM((IMAGES, COLUMNS), BF16),
            pltpu.VMEM((IMAGES, D), F32),
            pltpu.VMEM((ZLO, 2, QUARTER, WIDE), F32),
            pltpu.VMEM((COLUMNS, D), F32),
            pltpu.VMEM((4, GROUP, D), BF16),
            pltpu.VMEM((4, GROUP, D), BF16),
            pltpu.VMEM((6, GROUP // 2, D), BF16),
            pltpu.VMEM((6, GROUP // 2, D), BF16),
            pltpu.VMEM((3, PACKED, LANES), BF16),
            pltpu.VMEM((3, PACKED, LANES), BF16),
            pltpu.VMEM((15, QUARTER, WIDE), BF16),
            pltpu.VMEM((15, QUARTER, WIDE), BF16),
            pltpu.VMEM((NY, QUARTER + 8, LANES), F32),
            pltpu.VMEM((NY - 1, QUARTER + 8, LANES), F32),
            pltpu.VMEM((5, 8, LANES), F32),
            pltpu.VMEM((13, 8, LANES), F32),
            pltpu.SemaphoreType.DMA((COPIES,)),
            pltpu.SemaphoreType.DMA((COPIES,)),
            pltpu.SemaphoreType.DMA((4,)),
        ],
        compiler_params=pltpu.CompilerParams(
            collective_id=0, has_side_effects=True, vmem_limit_bytes=VMEM_LIMIT
        ),
    )(log_temp, bias, image_emb, text_emb)
    return (totals[0, :1], grad_image, grad_text, totals[2, :1], totals[1, :1])


def solution(mesh):
    return jax.shard_map(
        shards,
        mesh=mesh,
        in_specs=(P("grp", None), P(("blk", "grp"), None), P(), P()),
        out_specs=(P(), P("grp", "blk"), P(("blk", "grp"), None), P(), P()),
        check_vma=False,
    )
```

profile of v0, /device:TPU:6, one launch (start us, length us, event | category | flops | bytes accessed | tf_op | source)
XLA Modules:
  0.0 67.6 jit_solution(8175404229837621664)
XLA Ops:
  1.9 0.0 copy-start
  1.9 1.0 %copy-done = bf16[192,1152]{1,0:T(8,128)(2,1)S(1)} copy-done((bf16[192,1152]{1,0:T(8,128)(2,1)S(1)}, bf16[192,1152]{1,0:T(8,128)(2,1)}, u32[]{:S(2)}) %copy-start) | copy-done | bytes 442392
  2.9 0.0 copy-start.1
  2.9 0.8 %copy-done.1 = bf16[24,1152]{1,0:T(8,128)(2,1)S(1)} copy-done((bf16[24,1152]{1,0:T(8,128)(2,1)S(1)}, bf16[24,1152]{1,0:T(8,128)(2,1)}, u32[]{:S(2)}) %copy-start.1) | copy-done | bytes 55320
  3.8 61.9 %shard_map.83 = (f32[192,144]{1,0:T(8,128)S(1)}, f32[24,1152]{1,0:T(8,128)S(1)}, f32[8,128]{1,0:T(8,128)S(1)}) custom-call(f32[1]{0:T(128)S(6)} %copy.11.log_temp_in, f32[1]{0:T(128)S(6)} %copy.12.bias_in, bf16[192,1152]{1,0:T(8,128)(2,1)S(1)} %copy-done, bf16[24,1152]{1,0:T(8,128)(2,1)S(1)} %copy-done.1), custom_call_target="tpu_custom_call" | custom-call | tf_op jit(solution)/shard_map/pallas_call | solution.py:518
  65.7 0.5 fusion
  66.2 0.8 %copy.9 = f32[192,144]{0,1:T(8,128)} copy(f32[192,144]{1,0:T(8,128)S(1)} %get-tuple-element.12) | data formatting | bytes 221184
  67.0 0.6 copy.13
Async XLA Ops:
  1.9 1.0 %copy-start = (bf16[192,1152]{1,0:T(8,128)(2,1)S(1)}, bf16[192,1152]{1,0:T(8,128)(2,1)}, u32[]{:S(2)}) copy-start(bf16[192,1152]{1,0:T(8,128)(2,1)} %image_in.1) | copy-start | bytes 1327108
  2.9 0.8 %copy-start.1 = (bf16[24,1152]{1,0:T(8,128)(2,1)S(1)}, bf16[24,1152]{1,0:T(8,128)(2,1)}, u32[]{:S(2)}) copy-start(bf16[24,1152]{1,0:T(8,128)(2,1)} %text_in.1) | copy-start | bytes 165892
where the time goes:
time: 67.8 us; the launch traced here: 67.6 us
  Pallas kernels  61.9 us (91%)
  local copies, waits for them, and re-layouts  3.75 us (6%)
  between operations  1.94 us (3%)
    pallas_call x1, Pallas kernels, shards(): pl.pallas_call(kernel, out_shape=(jax.ShapeDtypeStruct((ROWS, SLOT), F32)...  61.9 us
    unnamed x6, local copies, waits for them, and re-layouts  3.23 us

commit v1 on v0

--- a/solution.py
+++ b/solution.py
@@ -55,16 +55,16 @@
 
     def first_axis(self, step):
         return self.at(
+            (self.x + step * self.core) % NX,
+            (self.y + step * (1 - self.core)) % NY,
+            self.z,
+            self.core,
+        )
+
+    def second_axis(self, step):
+        return self.at(
             (self.x + step * (1 - self.core)) % NX,
             (self.y + step * self.core) % NY,
-            self.z,
-            self.core,
-        )
-
-    def second_axis(self, step):
-        return self.at(
-            (self.x + step * self.core) % NX,
-            (self.y + step * (1 - self.core)) % NY,
             self.z,
             self.core,
         )
@@ -202,6 +202,15 @@
     images[0] = image[aligned(y * QUARTER, QUARTER), :]
     for copy in scalar_copies:
         copy.wait()
+    def image_ready(place):
+        rows = pl.ds(place * QUARTER, QUARTER)
+        values = images[place].astype(F32)
+        image_bf[rows, :] = (values * row_inverse(values)).astype(BF16)
+
+    image_ready(0)
+    quarters = [aligned(((y + k) % NY) * QUARTER, QUARTER) for k in range(NY)]
+    inverses = [row_inverse(image[rows, :].astype(F32)) for rows in quarters]
+
     pl.semaphore_wait(barrier, len(met))
 
     crossing, over_core, over_z = {}, {}, {}
@@ -229,11 +238,6 @@
     image_forward(0, 1)
     image_forward(0, -1)
     text_spread(0)
-
-    def image_ready(place):
-        rows = pl.ds(place * QUARTER, QUARTER)
-        values = images[place].astype(F32)
-        image_bf[rows, :] = (values * row_inverse(values)).astype(BF16)
 
     def texts_ready(texts, b, first):
         for half in range(2):
@@ -245,7 +249,6 @@
                 rows * row_inverse(rows)
             ).astype(BF16)
 
-    image_ready(0)
     for a in (1, 3, 2):
         crossing[a, 0].wait_recv()
         text_spread(a)
@@ -290,8 +293,8 @@
     block = (column * 2731) >> 16
     text_core = ((block >> 4) + core) & 1
     on_first, on_second = block & 3, (block >> 2) & 3
-    text_x = (x + jnp.where(text_core == 0, on_first, on_second)) & (NX - 1)
-    text_y = (y + jnp.where(text_core == 0, on_second, on_first)) & (NY - 1)
+    text_x = (x + jnp.where(text_core == 0, on_second, on_first)) & (NX - 1)
+    text_y = (y + jnp.where(text_core == 0, on_first, on_second)) & (NY - 1)
     text_ids = (
         ((z // ZLO) * NY + text_y) * (BATCH // 8)
         + ((text_x * ZLO + z % ZLO) * 2 + text_core) * TEXTS
@@ -439,9 +442,15 @@
     text_product(own_lanes)
     made = scalar_send(scalar_sum(made), [peers.along_y(step) for step in range(1, NY)])
 
-    def pair_sum(b):
-        pairs[b].wait_recv()
-        return text_part[pl.ds(b * GROUP, GROUP), :] + core_land[b].astype(F32)
+    ready = set()
+
+    def pair_sum(b, half):
+        if b not in ready:
+            pairs[b].wait_recv()
+            ready.add(b)
+        first = half * (GROUP // 2)
+        mine = text_part[pl.ds(b * GROUP + first, GROUP // 2), :]
+        return mine + core_land[b, pl.ds(first, GROUP // 2), :].astype(F32)
 
     across = {}
 
@@ -453,38 +462,31 @@
         across[at].wait_recv()
         return b_land[at].astype(F32)
 
-    low, high = slice(0, GROUP // 2), slice(GROUP // 2, GROUP)
-    opposite = pair_sum(2)
-    b_start(0, opposite[low], 1)
-    b_start(1, opposite[high], 3)
-    above, below = pair_sum(1), pair_sum(3)
-    b_start(2, above[high], 1)
-    b_start(3, below[low], 3)
-    text_sum = pair_sum(0)
+    b_start(0, pair_sum(2, 0), 1)
+    b_start(1, pair_sum(2, 1), 3)
+    b_start(2, pair_sum(1, 1), 1)
+    b_start(3, pair_sum(3, 0), 3)
     made = scalar_send(scalar_sum(made), [peers.along_z(step) for step in (4, 8, -4)])
     z_start(4)
-    b_start(4, above[low] + b_landed(0), 1)
-    b_start(5, below[high] + b_landed(1), 3)
+    b_start(4, pair_sum(1, 0) + b_landed(0), 1)
+    b_start(5, pair_sum(3, 1) + b_landed(1), 3)
     z_start(2)
-    text_sum = jnp.concatenate(
-        [
-            text_sum[low] + b_landed(3) + b_landed(4),
-            text_sum[high] + b_landed(2) + b_landed(5),
-        ],
-        axis=0,
-    )
     last = []
-    for a in (2, 1, 3):
-        a_send[a - 1] = pack(text_sum[a * TEXTS : (a + 1) * TEXTS, :]).astype(BF16)
+
+    def a_start(a, rows):
+        a_send[a - 1] = pack(rows).astype(BF16)
         last.append((copies.start(a_send.at[a - 1], a_land.at[3 - a], peers.first_axis(a)), 3 - a))
-    text_sum = pack(text_sum[:TEXTS, :])
+
+    rows = pair_sum(0, 1) + b_landed(2) + b_landed(5)
+    a_start(2, rows[:TEXTS])
+    a_start(3, rows[TEXTS:])
+    rows = pair_sum(0, 0) + b_landed(3) + b_landed(4)
+    a_start(1, rows[TEXTS:])
+    text_sum = pack(rows[:TEXTS])
     text_values = text[...].astype(F32)
     text_inverse = row_inverse(text_values)
     text_unit = text_values * text_inverse
     made = scalar_send(scalar_sum(made), [peers.along_z(step) for step in (1, 2, 3)])
-    quarters = [aligned(((y + k) % NY) * QUARTER, QUARTER) for k in range(NY)]
-    inverses = [row_inverse(image[rows, :].astype(F32)) for rows in quarters]
-
     grad = part(0)
     for side, most in Z_SIDES:
         grad = gathered(side, most, 0, grad)

time: 67.8 us -> 67.8 us (level); the launches traced: 67.6 us -> 66.5 us
  Pallas kernels: 61.9 us -> 60.8 us
    pallas_call x1, Pallas kernels: 61.9 us -> 60.8 us  [shards(): pl.pallas_call(kernel, out_shape=(jax.ShapeDtypeStruct((ROWS, SLOT), F32)...]
where the time goes in v1:
time: 67.8 us; the launch traced here: 66.5 us
  Pallas kernels  60.8 us (90%)
  local copies, waits for them, and re-layouts  3.75 us (6%)
  between operations  1.94 us (3%)
    pallas_call x1, Pallas kernels, shards(): pl.pallas_call(kernel, out_shape=(jax.ShapeDtypeStruct((ROWS, SLOT), F32)...  60.8 us
    unnamed x6, local copies, waits for them, and re-layouts  3.23 us

profile of v1, /device:TPU:6, one launch (start us, length us, event | category | flops | bytes accessed | tf_op | source)
XLA Modules:
  0.0 66.5 jit_solution(1836462866560405949)
XLA Ops:
  1.9 0.0 copy-start
  1.9 1.0 %copy-done = bf16[192,1152]{1,0:T(8,128)(2,1)S(1)} copy-done((bf16[192,1152]{1,0:T(8,128)(2,1)S(1)}, bf16[192,1152]{1,0:T(8,128)(2,1)}, u32[]{:S(2)}) %copy-start) | copy-done | bytes 442392
  2.9 0.0 copy-start.1
  2.9 0.8 %copy-done.1 = bf16[24,1152]{1,0:T(8,128)(2,1)S(1)} copy-done((bf16[24,1152]{1,0:T(8,128)(2,1)S(1)}, bf16[24,1152]{1,0:T(8,128)(2,1)}, u32[]{:S(2)}) %copy-start.1) | copy-done | bytes 55320
  3.8 60.8 %shard_map.83 = (f32[192,144]{1,0:T(8,128)S(1)}, f32[24,1152]{1,0:T(8,128)S(1)}, f32[8,128]{1,0:T(8,128)S(1)}) custom-call(f32[1]{0:T(128)S(6)} %copy.11.log_temp_in, f32[1]{0:T(128)S(6)} %copy.12.bias_in, bf16[192,1152]{1,0:T(8,128)(2,1)S(1)} %copy-done, bf16[24,1152]{1,0:T(8,128)(2,1)S(1)} %copy-done.1), custom_call_target="tpu_custom_call" | custom-call | tf_op jit(solution)/shard_map/pallas_call | solution.py:520
  64.6 0.5 fusion
  65.1 0.8 %copy.9 = f32[192,144]{0,1:T(8,128)} copy(f32[192,144]{1,0:T(8,128)S(1)} %get-tuple-element.12) | data formatting | bytes 221184
  65.9 0.6 copy.13
Async XLA Ops:
  1.9 1.0 %copy-start = (bf16[192,1152]{1,0:T(8,128)(2,1)S(1)}, bf16[192,1152]{1,0:T(8,128)(2,1)}, u32[]{:S(2)}) copy-start(bf16[192,1152]{1,0:T(8,128)(2,1)} %image_in.1) | copy-start | bytes 1327108
  2.9 0.8 %copy-start.1 = (bf16[24,1152]{1,0:T(8,128)(2,1)S(1)}, bf16[24,1152]{1,0:T(8,128)(2,1)}, u32[]{:S(2)}) copy-start(bf16[24,1152]{1,0:T(8,128)(2,1)} %text_in.1) | copy-start | bytes 165892

commit v2 on v1

--- a/solution.py
+++ b/solution.py
@@ -403,8 +403,8 @@
     others_ready(2)
     carry = weigh(0, NEAR, other_lanes, carry)
     image_grads(0, NEAR)
-    for far in (8, 7, 1):
-        z_start(far)
+    z_start(8)
+    z_start(7)
     for place in (3, 4, 5):
         image_ready(place)
     over_z[5].wait_recv()
@@ -436,8 +436,8 @@
         core_send[b] = text_part[pl.ds(OWN + b * GROUP, GROUP), :].astype(BF16)
         pairs[b] = copies.start(core_send.at[b], core_land.at[b], peers.other_core())
     image_grads(NEAR, ZLO)
-    for far in (6, 5, 3):
-        z_start(far)
+    z_start(6)
+    z_start(5)
     made = scalar_send(scalar_sum(made), [peers.along_x(step) for step in range(1, NX)])
     text_product(own_lanes)
     made = scalar_send(scalar_sum(made), [peers.along_y(step) for step in range(1, NY)])
@@ -468,9 +468,11 @@
     b_start(3, pair_sum(3, 0), 3)
     made = scalar_send(scalar_sum(made), [peers.along_z(step) for step in (4, 8, -4)])
     z_start(4)
+    z_start(3)
     b_start(4, pair_sum(1, 0) + b_landed(0), 1)
     b_start(5, pair_sum(3, 1) + b_landed(1), 3)
     z_start(2)
+    z_start(1)
     last = []
 
     def a_start(a, rows):

time: 67.8 us -> 69.3 us (1.022)
  Pallas kernels: 60.8 us -> 62.9 us
    pallas_call x1, Pallas kernels: 60.8 us -> 62.9 us  [shards(): pl.pallas_call(kernel, out_shape=(jax.ShapeDtypeStruct((ROWS, SLOT), F32)...]
where the time goes in v2:
time: 69.3 us; the launch traced here: 68.6 us
  Pallas kernels  62.9 us (91%)
  local copies, waits for them, and re-layouts  3.75 us (5%)
  between operations  1.94 us (3%)
    pallas_call x1, Pallas kernels, shards(): pl.pallas_call(kernel, out_shape=(jax.ShapeDtypeStruct((ROWS, SLOT), F32)...  62.9 us
    unnamed x6, local copies, waits for them, and re-layouts  3.23 us

profile of v2, /device:TPU:6, one launch (start us, length us, event | category | flops | bytes accessed | tf_op | source)
XLA Modules:
  0.0 68.6 jit_solution(4629523395623738387)
XLA Ops:
  1.9 0.0 copy-start
  1.9 1.0 %copy-done = bf16[192,1152]{1,0:T(8,128)(2,1)S(1)} copy-done((bf16[192,1152]{1,0:T(8,128)(2,1)S(1)}, bf16[192,1152]{1,0:T(8,128)(2,1)}, u32[]{:S(2)}) %copy-start) | copy-done | bytes 442392
  2.9 0.0 copy-start.1
  2.9 0.8 %copy-done.1 = bf16[24,1152]{1,0:T(8,128)(2,1)S(1)} copy-done((bf16[24,1152]{1,0:T(8,128)(2,1)S(1)}, bf16[24,1152]{1,0:T(8,128)(2,1)}, u32[]{:S(2)}) %copy-start.1) | copy-done | bytes 55320
  3.8 62.9 %shard_map.83 = (f32[192,144]{1,0:T(8,128)S(1)}, f32[24,1152]{1,0:T(8,128)S(1)}, f32[8,128]{1,0:T(8,128)S(1)}) custom-call(f32[1]{0:T(128)S(6)} %copy.11.log_temp_in, f32[1]{0:T(128)S(6)} %copy.12.bias_in, bf16[192,1152]{1,0:T(8,128)(2,1)S(1)} %copy-done, bf16[24,1152]{1,0:T(8,128)(2,1)S(1)} %copy-done.1), custom_call_target="tpu_custom_call" | custom-call | tf_op jit(solution)/shard_map/pallas_call | solution.py:522
  66.6 0.5 fusion
  67.1 0.8 %copy.9 = f32[192,144]{0,1:T(8,128)} copy(f32[192,144]{1,0:T(8,128)S(1)} %get-tuple-element.12) | data formatting | bytes 221184
  67.9 0.6 copy.13
Async XLA Ops:
  1.9 1.0 %copy-start = (bf16[192,1152]{1,0:T(8,128)(2,1)S(1)}, bf16[192,1152]{1,0:T(8,128)(2,1)}, u32[]{:S(2)}) copy-start(bf16[192,1152]{1,0:T(8,128)(2,1)} %image_in.1) | copy-start | bytes 1327108
  2.9 0.8 %copy-start.1 = (bf16[24,1152]{1,0:T(8,128)(2,1)S(1)}, bf16[24,1152]{1,0:T(8,128)(2,1)}, u32[]{:S(2)}) copy-start(bf16[24,1152]{1,0:T(8,128)(2,1)} %text_in.1) | copy-start | bytes 165892

commit v3 on v1

--- a/solution.py
+++ b/solution.py
@@ -344,7 +344,8 @@
     def image_grads(low, high):
         rows = pl.ds(low * QUARTER, (high - low) * QUARTER)
         grads[rows, :] = jnp.dot(weights[rows, :], text_bf[...], preferred_element_type=F32)
-        pl.loop(low, high)(project)
+        for place in range(low, high):
+            project(place)
 
     index = {}
     for side, most in Z_SIDES:

time: 67.8 us -> 66.7 us (0.984)
  the two profiles are of different devices: /device:TPU:6 before, /device:TPU:32 now
where the time goes in v3:
time: 66.7 us; the launch traced here: 66.5 us
  Pallas kernels  60.8 us (91%)
  local copies, waits for them, and re-layouts  3.75 us (6%)
  between operations  1.94 us (3%)
    pallas_call x1, Pallas kernels, shards(): pl.pallas_call(kernel, out_shape=(jax.ShapeDtypeStruct((ROWS, SLOT), F32)...  60.8 us
    unnamed x6, local copies, waits for them, and re-layouts  3.23 us

profile of v3, /device:TPU:32, one launch (start us, length us, event | category | flops | bytes accessed | tf_op | source)
XLA Modules:
  0.0 66.5 jit_solution(15312830436422186773)
XLA Ops:
  1.9 0.0 copy-start
  1.9 1.0 %copy-done = bf16[192,1152]{1,0:T(8,128)(2,1)S(1)} copy-done((bf16[192,1152]{1,0:T(8,128)(2,1)S(1)}, bf16[192,1152]{1,0:T(8,128)(2,1)}, u32[]{:S(2)}) %copy-start) | copy-done | bytes 442392
  2.9 0.0 copy-start.1
  2.9 0.8 %copy-done.1 = bf16[24,1152]{1,0:T(8,128)(2,1)S(1)} copy-done((bf16[24,1152]{1,0:T(8,128)(2,1)S(1)}, bf16[24,1152]{1,0:T(8,128)(2,1)}, u32[]{:S(2)}) %copy-start.1) | copy-done | bytes 55320
  3.8 60.8 %shard_map.83 = (f32[192,144]{1,0:T(8,128)S(1)}, f32[24,1152]{1,0:T(8,128)S(1)}, f32[8,128]{1,0:T(8,128)S(1)}) custom-call(f32[1]{0:T(128)S(6)} %copy.11.log_temp_in, f32[1]{0:T(128)S(6)} %copy.12.bias_in, bf16[192,1152]{1,0:T(8,128)(2,1)S(1)} %copy-done, bf16[24,1152]{1,0:T(8,128)(2,1)S(1)} %copy-done.1), custom_call_target="tpu_custom_call" | custom-call | tf_op jit(solution)/shard_map/pallas_call | solution.py:521
  64.6 0.5 fusion
  65.1 0.8 %copy.9 = f32[192,144]{0,1:T(8,128)} copy(f32[192,144]{1,0:T(8,128)S(1)} %get-tuple-element.12) | data formatting | bytes 221184
  65.9 0.6 copy.13
Async XLA Ops:
  1.9 1.0 %copy-start = (bf16[192,1152]{1,0:T(8,128)(2,1)S(1)}, bf16[192,1152]{1,0:T(8,128)(2,1)}, u32[]{:S(2)}) copy-start(bf16[192,1152]{1,0:T(8,128)(2,1)} %image_in.1) | copy-start | bytes 1327108
  2.9 0.8 %copy-start.1 = (bf16[24,1152]{1,0:T(8,128)(2,1)S(1)}, bf16[24,1152]{1,0:T(8,128)(2,1)}, u32[]{:S(2)}) copy-start(bf16[24,1152]{1,0:T(8,128)(2,1)} %text_in.1) | copy-start | bytes 165892
